TPU v7x, 256 devices: a whole 4x4x8 slice. The times are simulated.
256 devices in a mesh: lat: 16 (over x, z_lo, core), trc: 16 (over y, z_hi).
Axes of the slice: x: 4, y: 4, z: 8 (z_hi: 4, z_lo: 2; z = z_hi * 2 + z_lo), core: 2. Of those that a mesh axis runs over, the one named last changes fastest.
Arguments:
- tracers: float32 [128, 4, 128, 512], P('trc', None, 'lat'), may hold values from -6 to 6
- transports: float32 [2, 16, 3, 4, 128, 512], P(None, 'trc', None, None, 'lat'), may hold values from -0.1 to 0.1
- thickness: float32 [2, 16, 4, 128, 512], P(None, 'trc', None, 'lat'), may hold values from 1 to 2
- owner: int32 [2], replicated, may hold values from 0 to 15
- land_sea: int32 [128, 512], P('lat'), may hold values 0 or 1
- pairs: int32 [128], P('trc'), may hold values from 0 to 127, as said below
- rates: float32 [128], P('trc'), may hold values from 0.05 to 0.5
Outputs:
- result: float32 [128, 4, 128, 512], P('trc', None, 'lat')
Inputs may be any that keep to these rules, and one draw needn't show every extreme that they name: owner[s] is the index along trc whose record slot holds step s's transports and thicknesses. pairs[i] is a tracer other than i in the same group of 8 consecutive tracers as i, and every tracer is some tracer's partner.
All inputs are finite; a program needn't handle non-finite values. No bound on the sum of `land_sea` on one device may be relied on, other than what follows from the above.
Results may differ from a plain program's by a relative error of at most 0.0003.
Values sent between devices are 32-bit elements; how exact they have to be, the bound alone decides.
A program may use at most 64 MiB of HBM per device.

v0:
```python
import jax
import jax.numpy as jnp
from jax import lax
from jax.sharding import PartitionSpec as P


def with_halo(block, sides, width):
    for axis, dim in sides:
        count = lax.axis_size(axis)
        forward = [(i, i + 1) for i in range(count - 1)]
        backward = [(target, source) for source, target in forward]
        low = lax.ppermute(
            lax.slice_in_dim(block, block.shape[dim] - width, None, axis=dim), axis, forward
        )
        high = lax.ppermute(lax.slice_in_dim(block, 0, width, axis=dim), axis, backward)
        block = jnp.concatenate([low, block, high], axis=dim)
    return block


def broadcast(value, axis, source):
    kept = jnp.where(lax.axis_index(axis) == source, value, 0).astype(value.dtype)
    return lax.psum(kept, axis)


def cut_along(array, start_at, stop_at, along):
    return lax.slice_in_dim(array, start_at, stop_at, axis=array.ndim + along)


def ppm_sweep(tracer_pad, depth_pad, flows, along):
    count = flows.shape[flows.ndim + along] - 1
    left_cell = cut_along(tracer_pad, 1, count + 4, along)
    right_cell = cut_along(tracer_pad, 2, count + 5, along)
    edge_vals = 7.0 / 12.0 * (left_cell + right_cell) - 1.0 / 12.0 * (
        cut_along(tracer_pad, 0, count + 3, along) + cut_along(tracer_pad, 3, count + 6, along)
    )
    edge_vals = jnp.clip(
        edge_vals, jnp.minimum(left_cell, right_cell), jnp.maximum(left_cell, right_cell)
    )
    centre = cut_along(tracer_pad, 2, count + 4, along)
    left_dev = cut_along(edge_vals, 0, count + 2, along) - centre
    right_dev = cut_along(edge_vals, 1, count + 3, along) - centre
    left_lim = jnp.clip(left_dev, -2.0 * jnp.abs(right_dev), 2.0 * jnp.abs(right_dev))
    right_lim = jnp.clip(right_dev, -2.0 * jnp.abs(left_dev), 2.0 * jnp.abs(left_dev))
    left_edge = centre + left_lim
    right_edge = centre + right_lim
    slope_all = right_edge - left_edge
    curv_six = 6.0 * centre - 3.0 * (left_edge + right_edge)
    positive = flows > 0
    depth_up = jnp.where(
        positive,
        cut_along(depth_pad, 0, count + 1, along),
        cut_along(depth_pad, 1, count + 2, along),
    )
    courant = jnp.abs(flows) / jnp.maximum(depth_up, 0.25)
    from_left = cut_along(right_edge, 0, count + 1, along) - 0.5 * courant * (
        cut_along(slope_all, 0, count + 1, along)
        - (1.0 - 2.0 * courant / 3.0) * cut_along(curv_six, 0, count + 1, along)
    )
    from_right = cut_along(left_edge, 1, count + 2, along) + 0.5 * courant * (
        cut_along(slope_all, 1, count + 2, along)
        + (1.0 - 2.0 * courant / 3.0) * cut_along(curv_six, 1, count + 2, along)
    )
    flux_face = flows * jnp.where(positive, from_left, from_right)
    depth_old = cut_along(depth_pad, 1, count + 1, along)
    tracer_old = cut_along(tracer_pad, 3, count + 3, along)
    depth_new = (
        depth_old + cut_along(flows, 0, count, along) - cut_along(flows, 1, count + 1, along)
    )
    content = (
        depth_old * tracer_old
        + cut_along(flux_face, 0, count, along)
        - cut_along(flux_face, 1, count + 1, along)
    )
    return (content / depth_new, depth_new)


def zonal_and_vertical(field, depth, record, sea_mask):
    east_faces = record[0] * (sea_mask * jnp.roll(sea_mask, -1, axis=1))[None]
    flows = jnp.concatenate([east_faces[..., -1:], east_faces], axis=-1)
    tracer_pad = jnp.concatenate([field[..., -3:], field, field[..., :3]], axis=-1)
    depth_pad = jnp.concatenate([depth[..., -1:], depth, depth[..., :1]], axis=-1)
    field, depth = ppm_sweep(tracer_pad, depth_pad, flows, -1)
    tracer_pad = jnp.concatenate([field[:, :1]] * 3 + [field] + [field[:, -1:]] * 3, axis=1)
    depth_pad = jnp.concatenate([depth[:1], depth, depth[-1:]], axis=0)
    down_faces = record[2] * sea_mask[None]
    flows = jnp.concatenate([jnp.zeros_like(down_faces[:1]), down_faces], axis=0)
    field, depth = ppm_sweep(tracer_pad, depth_pad, flows, -3)
    return field


def meridional(field, record, sea_mask):
    north = record[1]
    depth = record[3]
    sea_plane = jnp.broadcast_to(sea_mask[None], depth.shape)
    tracer_pad = with_halo(field, (("lat", 2),), 3)
    small = jnp.stack([north, depth, sea_plane])
    small_pad = with_halo(small, (("lat", 2),), 1)
    north_rows = small_pad[0, :, 1:]
    depth_pad = small_pad[1]
    sea_rows = small_pad[2, 0]
    north_faces = north_rows * (sea_rows[:-1] * sea_rows[1:])[None]
    return ppm_sweep(tracer_pad, depth_pad, north_faces, -2)


def per_device(tracers, transports, thickness, owner, land_sea, pairs, rates):
    sea_mask = land_sea.astype(jnp.float32)
    group_size = tracers.shape[0]
    local_pairs = pairs - lax.axis_index("trc") * group_size
    chooser = (local_pairs[:, None] == jnp.arange(group_size, dtype=jnp.int32)[None, :]).astype(
        jnp.float32
    )
    field = tracers
    for step in range(transports.shape[0]):
        record = jnp.concatenate([transports[step, 0], thickness[step, 0][None]], axis=0)
        record = broadcast(record, "trc", owner[step])
        field, depth = meridional(field, record, sea_mask)
        field = zonal_and_vertical(field, depth, record, sea_mask)
        partner = jnp.einsum("ij,jlrc->ilrc", chooser, field, precision=lax.Precision.HIGHEST)
        field = field + sea_mask[None, None] * rates[:, None, None, None] * (partner - field)
    return field


def solution(mesh):
    placed = (
        P("trc", None, "lat", None),
        P(None, "trc", None, None, "lat", None),
        P(None, "trc", None, "lat", None),
        P(),
        P("lat", None),
        P("trc"),
        P("trc"),
    )
    return jax.shard_map(
        per_device,
        mesh=mesh,
        in_specs=placed,
        out_specs=P("trc", None, "lat", None),
        check_vma=False,
    )
```

profile of v0, /device:TPU:33, one launch (start us, length us, event | category | flops | bytes accessed | tf_op | source)
XLA Modules:
  0.0 236.3 jit_solution(14836258049032879893)
XLA Ops:
  6.5 1.3 copy.8
  7.9 3.4 %collective-permute-start.4 = (f32[8,4,3,512]{3,0,2,1:T(8,128)S(1)}, f32[8,4,3,512]{3,0,2,1:T(8,128)S(1)}, u32[]{:S(2)}, u32[]{:S(2)}) collective-permute-start(f32[8,4,3,512]{3,0,2,1:T(8,128)S(1)} %get-tuple-element.50), channel_id=1, source_target_pairs={{0,16},{16,32},{32,48},{48,64},{64,80},{80,96},{96,112},{112,128},... | collective-permute-start | bytes 589832 | tf_op jit(solution)/shard_map/ppermute | solution.py:12
  11.3 1.9 collective-permute-start.5
  13.3 0.6 copy-done.6
  14.0 0.6 fusion.163
  15.9 0.9 maximum_select_fusion
  16.9 0.6 copy-done.7
  17.7 0.6 copy-done.8
  18.3 0.3 constant_dynamic-update-slice_fusion.1
  18.6 0.6 collective-permute-done.5
  19.4 0.3 fusion.148
  20.0 157.4 %all-reduce.5.cloned.1.call-done = (f32[4,4,8,512]{3,2,1,0:T(8,128)}, f32[4,4,8,512]{3,2,1,0:T(8,128)}) async-done(((f32[4,4,8,512]{3,2,1,0:T(8,128)}, f32[4,4,8,512]{3,2,1,0:T(8,128)}), (f32[4,4,8,512]{3,2,1,0:T(8,128)}, f32[4,4,8,512]{3,2,1,0:T(8,128)})) %all-reduce.5.cloned.1.call-update) | async-done | bytes 524304 | tf_op jit(solution)/shard_map/psum | solution.py:22
  177.4 0.9 fusion.155
  178.5 12.9 %collective-permute-start.1 = (f32[3,4,1,512]{3,2,1,0:T(1,128)S(1)}, f32[3,4,1,512]{3,2,1,0:T(1,128)S(1)}, u32[]{:S(2)}, u32[]{:S(2)}) collective-permute-start(f32[3,4,1,512]{3,2,1,0:T(1,128)S(1)} %get-tuple-element.66), channel_id=1, source_target_pairs={{16,0},{32,16},{48,32},{64,48},{80,64},{96,80},{112,96},{128,112},... | collective-permute-start | bytes 73736 | tf_op jit(solution)/shard_map/ppermute | solution.py:15
  191.4 3.8 %collective-permute-start = (f32[3,4,1,512]{3,2,1,0:T(1,128)S(1)}, f32[3,4,1,512]{3,2,1,0:T(1,128)S(1)}, u32[]{:S(2)}, u32[]{:S(2)}) collective-permute-start(f32[3,4,1,512]{3,2,1,0:T(1,128)S(1)} %get-tuple-element.65), channel_id=1, source_target_pairs={{0,16},{16,32},{32,48},{48,64},{64,80},{80,96},{96,112},{112,128},... | collective-permute-start | bytes 73736 | tf_op jit(solution)/shard_map/ppermute | solution.py:12
  195.3 1.9 collective-permute-start.3
  197.2 4.5 %collective-permute-start.2 = (f32[3,4,1,512]{3,2,1,0:T(1,128)S(1)}, f32[3,4,1,512]{3,2,1,0:T(1,128)S(1)}, u32[]{:S(2)}, u32[]{:S(2)}) collective-permute-start(f32[3,4,1,512]{3,2,1,0:T(1,128)S(1)} %get-tuple-element.67), channel_id=1, source_target_pairs={{0,16},{16,32},{32,48},{48,64},{64,80},{80,96},{96,112},{112,128},... | collective-permute-start | bytes 73736 | tf_op jit(solution)/shard_map/ppermute | solution.py:12
  202.3 0.4 collective-permute-done.2
  203.3 0.4 fusion.80
  203.7 0.4 fusion.91
  204.2 0.3 pad_maximum_fusion.17
  204.5 0.6 fusion.63
  205.1 0.4 fusion.147
  205.7 0.3 multiply_subtract_fusion.4
  206.0 0.6 fusion.56
  206.7 0.3 fusion.90
  207.0 0.2 fusion.13
  207.2 0.4 fusion.145
  207.7 0.3 multiply_subtract_fusion.1
  208.0 0.5 fusion.48
  208.5 0.6 fusion.1
  209.1 5.1 %collective-permute-start.6 = (f32[8,4,3,512]{3,0,2,1:T(8,128)S(1)}, f32[8,4,3,512]{3,0,2,1:T(8,128)S(1)}, u32[]{:S(2)}, u32[]{:S(2)}) collective-permute-start(f32[8,4,3,512]{3,0,2,1:T(8,128)S(1)} %get-tuple-element.44), channel_id=1, source_target_pairs={{0,16},{16,32},{32,48},{48,64},{64,80},{80,96},{96,112},{112,128},... | collective-permute-start | bytes 589832 | tf_op jit(solution)/shard_map/ppermute | solution.py:12
  214.2 2.1 collective-permute-start.7
  216.6 2.2 collective-permute-done.6
  218.8 3.3 %collective-permute-done.7 = f32[8,4,3,512]{3,0,2,1:T(8,128)S(1)} collective-permute-done((f32[8,4,3,512]{3,0,2,1:T(8,128)S(1)}, f32[8,4,3,512]{3,0,2,1:T(8,128)S(1)}, u32[]{:S(2)}, u32[]{:S(2)}) %collective-permute-start.7) | collective-permute-done | bytes 196640 | tf_op jit(solution)/shard_map/ppermute | solution.py:15
  222.4 0.3 fusion.143
  223.0 0.4 fusion.72
  223.7 0.3 pad_maximum_fusion.18
  224.0 0.6 fusion.67
  224.6 0.4 fusion.142
  225.0 0.3 multiply_subtract_fusion.2
  225.3 0.6 fusion.40
  226.0 0.3 fusion.86
  226.6 0.4 fusion.140
  227.0 0.3 multiply_subtract_fusion
  227.3 0.5 fusion.32
  227.8 0.6 fusion.3
  228.4 1.1 copy.14
  (77 shorter events, 3.7 us)
Async XLA Ops:
  6.5 170.9 %all-reduce.5.cloned.1.call-start = ((), (), s32[]{:S(2)}) async-start(), calls=%async_computation | async-start | bytes 1048576 | tf_op jit(solution)/shard_map/psum | solution.py:22
  7.9 5.4 %copy-start.4 = (f32[2,1,4,8,512]{4,3,2,1,0:T(8,128)S(1)}, f32[2,1,4,8,512]{4,3,2,1,0:T(8,128)}, u32[]{:S(2)}) copy-start(f32[2,1,4,8,512]{4,3,2,1,0:T(8,128)} %param.9) | copy-start | bytes 393220
  7.9 5.4 %copy-start.1 = (f32[2,1,3,4,8,512]{5,4,3,2,1,0:T(8,128)S(1)}, f32[2,1,3,4,8,512]{5,4,3,2,1,0:T(8,128)}, u32[]{:S(2)}) copy-start(f32[2,1,3,4,8,512]{5,4,3,2,1,0:T(8,128)} %param.8) | copy-start | bytes 1179652
  7.9 10.3 %collective-permute-start.4 = (f32[8,4,3,512]{3,0,2,1:T(8,128)S(1)}, f32[8,4,3,512]{3,0,2,1:T(8,128)S(1)}, u32[]{:S(2)}, u32[]{:S(2)}) collective-permute-start(f32[8,4,3,512]{3,0,2,1:T(8,128)S(1)} %get-tuple-element.50), channel_id=1, source_target_pairs={{0,16},{16,32},{32,48},{48,64},{64,80},{80,96},{96,112},{112,128},... | collective-permute-start | bytes 589832 | tf_op jit(solution)/shard_map/ppermute | solution.py:12
  11.3 7.9 %collective-permute-start.5 = (f32[8,4,3,512]{3,0,2,1:T(8,128)S(1)}, f32[8,4,3,512]{3,0,2,1:T(8,128)S(1)}, u32[]{:S(2)}, u32[]{:S(2)}) collective-permute-start(f32[8,4,3,512]{3,0,2,1:T(8,128)S(1)} %get-tuple-element.49), channel_id=1, source_target_pairs={{16,0},{32,16},{48,32},{64,48},{80,64},{96,80},{112,96},{128,112},... | collective-permute-start | bytes 589832 | tf_op jit(solution)/shard_map/ppermute | solution.py:15
  13.3 0.7 copy-start.6
  15.9 0.9 copy-start.5
  16.7 1.5 copy-start
  16.8 0.7 copy-start.7
  17.6 0.7 copy-start.8
  177.4 1.0 copy-start.2
  178.5 23.3 %copy-start.3 = (f32[4,4,8,512]{3,2,1,0:T(8,128)S(1)}, f32[4,4,8,512]{3,2,1,0:T(8,128)}, u32[]{:S(2)}) copy-start(f32[4,4,8,512]{3,2,1,0:T(8,128)} %get-tuple-element.6) | copy-start | bytes 786436
  178.5 23.6 %collective-permute-start.1 = (f32[3,4,1,512]{3,2,1,0:T(1,128)S(1)}, f32[3,4,1,512]{3,2,1,0:T(1,128)S(1)}, u32[]{:S(2)}, u32[]{:S(2)}) collective-permute-start(f32[3,4,1,512]{3,2,1,0:T(1,128)S(1)} %get-tuple-element.66), channel_id=1, source_target_pairs={{16,0},{32,16},{48,32},{64,48},{80,64},{96,80},{112,96},{128,112},... | collective-permute-start | bytes 73736 | tf_op jit(solution)/shard_map/ppermute | solution.py:15
  191.4 10.9 %collective-permute-start = (f32[3,4,1,512]{3,2,1,0:T(1,128)S(1)}, f32[3,4,1,512]{3,2,1,0:T(1,128)S(1)}, u32[]{:S(2)}, u32[]{:S(2)}) collective-permute-start(f32[3,4,1,512]{3,2,1,0:T(1,128)S(1)} %get-tuple-element.65), channel_id=1, source_target_pairs={{0,16},{16,32},{32,48},{48,64},{64,80},{80,96},{96,112},{112,128},... | collective-permute-start | bytes 73736 | tf_op jit(solution)/shard_map/ppermute | solution.py:12
  195.3 6.9 %collective-permute-start.3 = (f32[3,4,1,512]{3,2,1,0:T(1,128)S(1)}, f32[3,4,1,512]{3,2,1,0:T(1,128)S(1)}, u32[]{:S(2)}, u32[]{:S(2)}) collective-permute-start(f32[3,4,1,512]{3,2,1,0:T(1,128)S(1)} %get-tuple-element.68), channel_id=1, source_target_pairs={{16,0},{32,16},{48,32},{64,48},{80,64},{96,80},{112,96},{128,112},... | collective-permute-start | bytes 73736 | tf_op jit(solution)/shard_map/ppermute | solution.py:15
  197.2 5.5 %collective-permute-start.2 = (f32[3,4,1,512]{3,2,1,0:T(1,128)S(1)}, f32[3,4,1,512]{3,2,1,0:T(1,128)S(1)}, u32[]{:S(2)}, u32[]{:S(2)}) collective-permute-start(f32[3,4,1,512]{3,2,1,0:T(1,128)S(1)} %get-tuple-element.67), channel_id=1, source_target_pairs={{0,16},{16,32},{32,48},{48,64},{64,80},{80,96},{96,112},{112,128},... | collective-permute-start | bytes 73736 | tf_op jit(solution)/shard_map/ppermute | solution.py:12
  209.1 9.7 %collective-permute-start.6 = (f32[8,4,3,512]{3,0,2,1:T(8,128)S(1)}, f32[8,4,3,512]{3,0,2,1:T(8,128)S(1)}, u32[]{:S(2)}, u32[]{:S(2)}) collective-permute-start(f32[8,4,3,512]{3,0,2,1:T(8,128)S(1)} %get-tuple-element.44), channel_id=1, source_target_pairs={{0,16},{16,32},{32,48},{48,64},{64,80},{80,96},{96,112},{112,128},... | collective-permute-start | bytes 589832 | tf_op jit(solution)/shard_map/ppermute | solution.py:12
  214.2 7.9 %collective-permute-start.7 = (f32[8,4,3,512]{3,0,2,1:T(8,128)S(1)}, f32[8,4,3,512]{3,0,2,1:T(8,128)S(1)}, u32[]{:S(2)}, u32[]{:S(2)}) collective-permute-start(f32[8,4,3,512]{3,0,2,1:T(8,128)S(1)} %get-tuple-element.43), channel_id=1, source_target_pairs={{16,0},{32,16},{48,32},{64,48},{80,64},{96,80},{112,96},{128,112},... | collective-permute-start | bytes 589832 | tf_op jit(solution)/shard_map/ppermute | solution.py:15
Sparse Core Ops, SparseCore 0:
  16.9 160.4 all-reduce.4
where the time goes:
time: 237 us; the launch traced here: 236 us
  waiting for transfers between devices  164 us (69%)
  starting transfers between devices  35.6 us (15%)
  between operations  15.4 us (6%)
  other arithmetic  13.2 us (6%)
  local copies, waits for them, and re-layouts  7.03 us (3%)
    psum x1, waiting for transfers between devices, broadcast(): return lax.psum(kept, axis)  157 us
    ppermute x4, starting transfers between devices, with_halo(): lax.ppermute(lax.slice_in_dim(block, 0, width, axis=dim), axis, backward)  18.8 us
    ppermute x4, starting transfers between devices, with_halo(): lax.ppermute(lax.slice_in_dim(block, block.shape[dim] - width, None, axis...  16.8 us
  transfers between devices with their start and end apart: 9, of which 5 were waited for; matrix products, arithmetic and copies ran while one was open for 2% of the time, Pallas kernels for 0%

commit v1 on v0

--- a/solution.py
+++ b/solution.py
@@ -19,7 +19,7 @@
 
 def broadcast(value, axis, source):
     kept = jnp.where(lax.axis_index(axis) == source, value, 0).astype(value.dtype)
-    return lax.psum(kept, axis)
+    return jnp.sum(lax.all_gather(kept, axis), axis=0)
 
 
 def cut_along(array, start_at, stop_at, along):

time: 237 us -> 223 us (0.941); the launches traced: 236 us -> 220 us
  waiting for transfers between devices: 164 us -> 149 us
  starting transfers between devices: 35.6 us -> 24.1 us
  other arithmetic: 13.2 us -> 22.2 us
    psum x1 -> x0, waiting for transfers between devices: 157 us -> none  [broadcast(): return lax.psum(kept, axis)]
    all_gather x0 -> x2, waiting for transfers between devices: none -> 142 us  [broadcast(): return jnp.sum(lax.all_gather(kept, axis), axis=0)]
    ppermute x4, starting transfers between devices: 18.8 us -> 8.58 us  [with_halo(): lax.ppermute(lax.slice_in_dim(block, 0, width, axis=dim), axis, backward)]
    reduce_sum x0 -> x2, other arithmetic: none -> 5.97 us  [broadcast(): return jnp.sum(lax.all_gather(kept, axis), axis=0)]
  transfers between devices with their start and end apart: 9 -> 10, of which waited for: 5 -> 6; matrix products, arithmetic and copies ran while one was open for 2% -> 4% of each run, Pallas kernels for 0% -> 0%
where the time goes in v1:
time: 223 us; the launch traced here: 220 us
  waiting for transfers between devices  149 us (67%)
  starting transfers between devices  24.1 us (11%)
  other arithmetic  22.2 us (10%)
  between operations  15.3 us (7%)
  local copies, waits for them, and re-layouts  7.76 us (3%)
    all_gather x2, waiting for transfers between devices, broadcast(): return jnp.sum(lax.all_gather(kept, axis), axis=0)  142 us
    ppermute x4, starting transfers between devices, with_halo(): lax.ppermute(lax.slice_in_dim(block, block.shape[dim] - width, None, axis...  15.4 us
    ppermute x4, starting transfers between devices, with_halo(): lax.ppermute(lax.slice_in_dim(block, 0, width, axis=dim), axis, backward)  8.58 us
    reduce_sum x2, other arithmetic, broadcast(): return jnp.sum(lax.all_gather(kept, axis), axis=0)  5.97 us
    ppermute x4, waiting for transfers between devices, with_halo(): lax.ppermute(lax.slice_in_dim(block, 0, width, axis=dim), axis, backward)  5.47 us
  transfers between devices with their start and end apart: 10, of which 6 were waited for; matrix products, arithmetic and copies ran while one was open for 4% of the time, Pallas kernels for 0%

profile of v1, /device:TPU:33, one launch (start us, length us, event | category | flops | bytes accessed | tf_op | source)
XLA Modules:
  0.0 219.6 jit_solution(15611605108806224373)
XLA Ops:
  6.6 1.3 fusion.164
  7.9 0.9 fusion.159
  8.8 1.1 slice_bitcast_fusion.1
  10.5 0.7 maximum_select_fusion
  11.9 0.8 maximum_select_fusion.1
  12.7 1.4 copy.15
  14.1 2.6 %collective-permute-start.5 = (f32[8,4,3,512]{3,0,2,1:T(8,128)S(1)}, f32[8,4,3,512]{3,0,2,1:T(8,128)S(1)}, u32[]{:S(2)}, u32[]{:S(2)}) collective-permute-start(f32[8,4,3,512]{3,0,2,1:T(8,128)S(1)} %get-tuple-element.47), channel_id=1, source_target_pairs={{16,0},{32,16},{48,32},{64,48},{80,64},{96,80},{112,96},{128,112},... | collective-permute-start | bytes 589832 | tf_op jit(solution)/shard_map/ppermute | solution.py:15
  16.7 3.9 %collective-permute-start.4 = (f32[8,4,3,512]{3,0,2,1:T(8,128)S(1)}, f32[8,4,3,512]{3,0,2,1:T(8,128)S(1)}, u32[]{:S(2)}, u32[]{:S(2)}) collective-permute-start(f32[8,4,3,512]{3,0,2,1:T(8,128)S(1)} %get-tuple-element.48), channel_id=1, source_target_pairs={{0,16},{16,32},{32,48},{48,64},{64,80},{80,96},{96,112},{112,128},... | collective-permute-start | bytes 589832 | tf_op jit(solution)/shard_map/ppermute | solution.py:12
  20.7 0.7 maximum_multiply_fusion
  21.3 0.7 broadcast_multiply_fusion
  22.1 0.5 broadcast_subtract_fusion
  22.6 0.5 collective-permute-done.4
  23.2 0.3 constant_dynamic-update-slice_fusion.1
  23.8 0.3 fusion.148
  24.3 66.8 %all-gather.3.cloned.1.call-done = f32[16,4,4,8,512]{4,3,2,1,0:T(8,128)} async-done(((f32[1,4,4,8,512]{4,3,2,1,0:T(8,128)}), f32[16,4,4,8,512]{4,3,2,1,0:T(8,128)}) %all-gather.3.cloned.1.call-update) | async-done | bytes 4194320 | tf_op jit(solution)/shard_map/all_gather | solution.py:22
  91.1 2.6 %reduce_sum.18 = f32[4,4,8,512]{3,2,1,0:T(8,128)S(1)} reduce(f32[16,4,4,8,512]{4,3,2,1,0:T(8,128)} %all-gather.3.cloned.1.call-done, f32[]{:T(128)} %constant.15.clone.1), dimensions={0}, to_apply=%region_0.1 | reduce | flops 983040 | bytes 4456452 | tf_op jit(solution)/shard_map/reduce_sum | solution.py:22
  93.8 75.6 %all-gather.5.cloned.1.call-done = f32[16,4,4,8,512]{4,3,2,1,0:T(8,128)} async-done(((f32[1,4,4,8,512]{4,3,2,1,0:T(8,128)}), f32[16,4,4,8,512]{4,3,2,1,0:T(8,128)}) %all-gather.5.cloned.1.call-update) | async-done | bytes 4194320 | tf_op jit(solution)/shard_map/all_gather | solution.py:22
  169.3 3.3 %reduce_sum.19 = f32[4,4,8,512]{3,2,1,0:T(8,128)} reduce(f32[16,4,4,8,512]{4,3,2,1,0:T(8,128)} %all-gather.5.cloned.1.call-done, f32[]{:T(128)} %constant.15.clone.1), dimensions={0}, to_apply=%region_1.2 | reduce | flops 983040 | bytes 4456452 | tf_op jit(solution)/shard_map/reduce_sum | solution.py:22
  172.7 0.9 fusion.156
  173.5 0.9 fusion.126
  174.7 2.5 %collective-permute-start = (f32[3,4,1,512]{3,2,1,0:T(1,128)S(1)}, f32[3,4,1,512]{3,2,1,0:T(1,128)S(1)}, u32[]{:S(2)}, u32[]{:S(2)}) collective-permute-start(f32[3,4,1,512]{3,2,1,0:T(1,128)S(1)} %get-tuple-element.63), channel_id=1, source_target_pairs={{0,16},{16,32},{32,48},{48,64},{64,80},{80,96},{96,112},{112,128},... | collective-permute-start | bytes 73736 | tf_op jit(solution)/shard_map/ppermute | solution.py:12
  177.2 2.2 collective-permute-start.1
  179.4 4.3 %collective-permute-start.2 = (f32[3,4,1,512]{3,2,1,0:T(1,128)S(1)}, f32[3,4,1,512]{3,2,1,0:T(1,128)S(1)}, u32[]{:S(2)}, u32[]{:S(2)}) collective-permute-start(f32[3,4,1,512]{3,2,1,0:T(1,128)S(1)} %get-tuple-element.65), channel_id=1, source_target_pairs={{0,16},{16,32},{32,48},{48,64},{64,80},{80,96},{96,112},{112,128},... | collective-permute-start | bytes 73736 | tf_op jit(solution)/shard_map/ppermute | solution.py:12
  183.7 1.9 collective-permute-start.3
  185.8 4.0 %collective-permute-done.3 = f32[3,4,1,512]{3,2,1,0:T(1,128)S(1)} collective-permute-done((f32[3,4,1,512]{3,2,1,0:T(1,128)S(1)}, f32[3,4,1,512]{3,2,1,0:T(1,128)S(1)}, u32[]{:S(2)}, u32[]{:S(2)}) %collective-permute-start.3) | collective-permute-done | bytes 24608 | tf_op jit(solution)/shard_map/ppermute | solution.py:15
  190.6 0.4 fusion.80
  191.0 0.4 fusion.91
  191.8 0.6 fusion.63
  192.4 0.4 fusion.147
  193.2 0.6 fusion.56
  193.8 0.3 fusion.90
  194.4 0.4 fusion.145
  195.2 0.5 fusion.48
  195.7 0.6 fusion.1
  196.3 1.9 collective-permute-start.7
  198.3 4.7 %collective-permute-start.6 = (f32[8,4,3,512]{3,0,2,1:T(8,128)S(1)}, f32[8,4,3,512]{3,0,2,1:T(8,128)S(1)}, u32[]{:S(2)}, u32[]{:S(2)}) collective-permute-start(f32[8,4,3,512]{3,0,2,1:T(8,128)S(1)} %get-tuple-element.42), channel_id=1, source_target_pairs={{0,16},{16,32},{32,48},{48,64},{64,80},{80,96},{96,112},{112,128},... | collective-permute-start | bytes 589832 | tf_op jit(solution)/shard_map/ppermute | solution.py:12
  203.2 1.5 collective-permute-done.7
  204.7 0.7 collective-permute-done.6
  205.7 0.3 fusion.143
  206.3 0.4 fusion.72
  207.2 0.6 fusion.67
  207.8 0.4 fusion.142
  208.6 0.6 fusion.40
  209.2 0.3 fusion.86
  209.8 0.4 fusion.140
  210.5 0.5 fusion.32
  211.0 0.6 fusion.3
  211.6 1.1 copy.21
  (74 shorter events, 5.3 us)
Async XLA Ops:
  6.5 16.6 %copy-start = (f32[8,4,8,512]{3,2,1,0:T(8,128)S(1)}, f32[8,4,8,512]{3,2,1,0:T(8,128)}, u32[]{:S(2)}) copy-start(f32[8,4,8,512]{3,2,1,0:T(8,128)} %param.7) | copy-start | bytes 1572868
  6.5 14.0 %copy-start.2 = (s32[8,512]{1,0:T(8,128)S(1)}, s32[8,512]{1,0:T(8,128)}, u32[]{:S(2)}) copy-start(s32[8,512]{1,0:T(8,128)} %param.11) | copy-start | bytes 49156
  6.5 14.8 %copy-start.3 = (f32[8]{0:T(128)S(1)}, f32[8]{0:T(128)}, u32[]{:S(2)}) copy-start(f32[8]{0:T(128)} %param.13) | copy-start | bytes 100
  6.5 15.5 %copy-start.4 = (s32[8]{0:T(128)S(1)}, s32[8]{0:T(128)}, u32[]{:S(2)}) copy-start(s32[8]{0:T(128)} %param.12) | copy-start | bytes 100
  6.5 84.6 %all-gather.3.cloned.1.call-start = ((), (), s32[]{:S(2)}) async-start(), calls=%async_computation | async-start | bytes 4456448 | tf_op jit(solution)/shard_map/all_gather | solution.py:22
  11.2 158.1 %all-gather.5.cloned.1.call-start = ((), (), s32[]{:S(2)}) async-start(), calls=%async_computation.1 | async-start | bytes 4456448 | tf_op jit(solution)/shard_map/all_gather | solution.py:22
  14.1 9.4 %collective-permute-start.5 = (f32[8,4,3,512]{3,0,2,1:T(8,128)S(1)}, f32[8,4,3,512]{3,0,2,1:T(8,128)S(1)}, u32[]{:S(2)}, u32[]{:S(2)}) collective-permute-start(f32[8,4,3,512]{3,0,2,1:T(8,128)S(1)} %get-tuple-element.47), channel_id=1, source_target_pairs={{16,0},{32,16},{48,32},{64,48},{80,64},{96,80},{112,96},{128,112},... | collective-permute-start | bytes 589832 | tf_op jit(solution)/shard_map/ppermute | solution.py:15
  16.7 6.5 %collective-permute-start.4 = (f32[8,4,3,512]{3,0,2,1:T(8,128)S(1)}, f32[8,4,3,512]{3,0,2,1:T(8,128)S(1)}, u32[]{:S(2)}, u32[]{:S(2)}) collective-permute-start(f32[8,4,3,512]{3,0,2,1:T(8,128)S(1)} %get-tuple-element.48), channel_id=1, source_target_pairs={{0,16},{16,32},{32,48},{48,64},{64,80},{80,96},{96,112},{112,128},... | collective-permute-start | bytes 589832 | tf_op jit(solution)/shard_map/ppermute | solution.py:12
  174.7 15.2 %collective-permute-start = (f32[3,4,1,512]{3,2,1,0:T(1,128)S(1)}, f32[3,4,1,512]{3,2,1,0:T(1,128)S(1)}, u32[]{:S(2)}, u32[]{:S(2)}) collective-permute-start(f32[3,4,1,512]{3,2,1,0:T(1,128)S(1)} %get-tuple-element.63), channel_id=1, source_target_pairs={{0,16},{16,32},{32,48},{48,64},{64,80},{80,96},{96,112},{112,128},... | collective-permute-start | bytes 73736 | tf_op jit(solution)/shard_map/ppermute | solution.py:12
  177.2 8.6 %collective-permute-start.1 = (f32[3,4,1,512]{3,2,1,0:T(1,128)S(1)}, f32[3,4,1,512]{3,2,1,0:T(1,128)S(1)}, u32[]{:S(2)}, u32[]{:S(2)}) collective-permute-start(f32[3,4,1,512]{3,2,1,0:T(1,128)S(1)} %get-tuple-element.64), channel_id=1, source_target_pairs={{16,0},{32,16},{48,32},{64,48},{80,64},{96,80},{112,96},{128,112},... | collective-permute-start | bytes 73736 | tf_op jit(solution)/shard_map/ppermute | solution.py:15
  179.4 10.5 %collective-permute-start.2 = (f32[3,4,1,512]{3,2,1,0:T(1,128)S(1)}, f32[3,4,1,512]{3,2,1,0:T(1,128)S(1)}, u32[]{:S(2)}, u32[]{:S(2)}) collective-permute-start(f32[3,4,1,512]{3,2,1,0:T(1,128)S(1)} %get-tuple-element.65), channel_id=1, source_target_pairs={{0,16},{16,32},{32,48},{48,64},{64,80},{80,96},{96,112},{112,128},... | collective-permute-start | bytes 73736 | tf_op jit(solution)/shard_map/ppermute | solution.py:12
  183.7 6.0 %collective-permute-start.3 = (f32[3,4,1,512]{3,2,1,0:T(1,128)S(1)}, f32[3,4,1,512]{3,2,1,0:T(1,128)S(1)}, u32[]{:S(2)}, u32[]{:S(2)}) collective-permute-start(f32[3,4,1,512]{3,2,1,0:T(1,128)S(1)} %get-tuple-element.66), channel_id=1, source_target_pairs={{16,0},{32,16},{48,32},{64,48},{80,64},{96,80},{112,96},{128,112},... | collective-permute-start | bytes 73736 | tf_op jit(solution)/shard_map/ppermute | solution.py:15
  194.8 0.9 copy-start.1
  194.8 0.9 copy-start.5
  196.3 8.4 %collective-permute-start.7 = (f32[8,4,3,512]{3,0,2,1:T(8,128)S(1)}, f32[8,4,3,512]{3,0,2,1:T(8,128)S(1)}, u32[]{:S(2)}, u32[]{:S(2)}) collective-permute-start(f32[8,4,3,512]{3,0,2,1:T(8,128)S(1)} %get-tuple-element.41), channel_id=1, source_target_pairs={{16,0},{32,16},{48,32},{64,48},{80,64},{96,80},{112,96},{128,112},... | collective-permute-start | bytes 589832 | tf_op jit(solution)/shard_map/ppermute | solution.py:15
  198.3 7.1 %collective-permute-start.6 = (f32[8,4,3,512]{3,0,2,1:T(8,128)S(1)}, f32[8,4,3,512]{3,0,2,1:T(8,128)S(1)}, u32[]{:S(2)}, u32[]{:S(2)}) collective-permute-start(f32[8,4,3,512]{3,0,2,1:T(8,128)S(1)} %get-tuple-element.42), channel_id=1, source_target_pairs={{0,16},{16,32},{32,48},{48,64},{64,80},{80,96},{96,112},{112,128},... | collective-permute-start | bytes 589832 | tf_op jit(solution)/shard_map/ppermute | solution.py:12
Sparse Core Ops, SparseCore 0:
  11.4 79.7 all-gather.2
  93.5 75.7 all-gather.4
